TPU v7x, 512 devices: a whole 4x4x16 slice. The times are simulated.
512 devices in a mesh: group: 8 (over x, core), dev: 64 (over z, y).
Axes of the slice: x: 4, y: 4, z: 16, core: 2. Of those that a mesh axis runs over, the one named last changes fastest.
Arguments:
- cam_jac: float32 [2, 9, 8, 262144], P(None, None, None, ('group', 'dev')), may hold values from -6 to 6
- lm_jac: float32 [2, 3, 8, 262144], P(None, None, None, ('group', 'dev')), may hold values from -6 to 6
- resid: float32 [2, 8, 262144], P(None, None, ('group', 'dev')), may hold values from -6 to 6
- cam_index: int32 [8, 262144], P(None, ('group', 'dev')), may hold values from 0 to 8191
Outputs:
- camera_step: float32 [9, 8192], P(None, 'dev')
- camera_residual: float32 [9, 8192], P(None, 'dev')
- landmark_step: float32 [3, 262144], P(None, ('group', 'dev'))
Inputs may be any that keep to these rules, and one draw needn't show every extreme that they name: `cam_index`: every observation names one of the 8192 cameras.
All inputs are finite; a program needn't handle non-finite values.
Results may differ from a plain program's by a relative error of at most 0.0003.
Values sent between devices are 32-bit elements; how exact they have to be, the bound alone decides.
A program may use at most 64 MiB of HBM per device.

v0:
```python
import jax
import jax.numpy as jnp
from jax import lax
from jax.sharding import PartitionSpec as P

CAM_DEV = 128
ITERS = 2
DAMPING = 1.0


def landmark_inverse(lm_jac):

    def entry(first, second):
        return jnp.sum(lm_jac[:, first] * lm_jac[:, second], axis=(0, 1))

    w_00 = entry(0, 0) + DAMPING
    w_11 = entry(1, 1) + DAMPING
    w_22 = entry(2, 2) + DAMPING
    w_01 = entry(0, 1)
    w_02 = entry(0, 2)
    w_12 = entry(1, 2)
    cof_00 = w_11 * w_22 - w_12 * w_12
    cof_01 = w_02 * w_12 - w_01 * w_22
    cof_02 = w_01 * w_12 - w_02 * w_11
    cof_11 = w_00 * w_22 - w_02 * w_02
    cof_12 = w_01 * w_02 - w_00 * w_12
    cof_22 = w_00 * w_11 - w_01 * w_01
    determinant = w_00 * cof_00 + w_01 * cof_01 + w_02 * cof_02
    rows = [
        jnp.stack([cof_00, cof_01, cof_02]),
        jnp.stack([cof_01, cof_11, cof_12]),
        jnp.stack([cof_02, cof_12, cof_22]),
    ]
    return jnp.stack(rows) / determinant[None, None]


def apply_inverse(inverse, vector):
    return jnp.sum(inverse * vector[None], axis=1)


def landmark_side(lm_jac, values):
    return jnp.sum(lm_jac * values[:, None], axis=(0, 2))


def back_project(lm_jac, landmark):
    return jnp.sum(lm_jac * landmark[None, :, None, :], axis=1)


def camera_apply(cam_jac, cam_values):
    return jnp.sum(cam_jac * cam_values[None], axis=1)


def camera_transpose(cam_jac, errors):
    return jnp.sum(cam_jac * errors[:, None], axis=0)


def to_cameras(values, cam_index, total_cams):
    flat_index = cam_index.reshape(-1)
    width = values.shape[0]

    def one_row(column):
        return jax.ops.segment_sum(column, flat_index, num_segments=total_cams)

    return jax.vmap(one_row)(values.reshape(width, -1))


def schur_obs(cam_jac, lm_jac, inverse, cam_values):
    applied = camera_apply(cam_jac, cam_values)
    landmark = apply_inverse(inverse, landmark_side(lm_jac, applied))
    return camera_transpose(cam_jac, applied - back_project(lm_jac, landmark))


def gather_cameras(tile):
    return lax.all_gather(tile, "dev", axis=1, tiled=True)


def reduce_cameras(terms):
    totals = lax.psum(terms, ("group", "dev"))
    width = terms.shape[1] // lax.axis_size("dev")
    return lax.dynamic_slice_in_dim(totals, lax.axis_index("dev") * width, width, 1)


def inner_product(left, right):
    return lax.psum(jnp.sum(left * right), "dev")


def body(cam_jac, lm_jac, resid, cam_index):
    total_cams = CAM_DEV * lax.axis_size("dev")
    inverse = landmark_inverse(lm_jac)
    land_rhs = apply_inverse(inverse, landmark_side(lm_jac, resid))
    errors = resid - back_project(lm_jac, land_rhs)
    stacked = jnp.concatenate(
        [camera_transpose(cam_jac, errors), jnp.sum(cam_jac * cam_jac, axis=0)], axis=0
    )
    summed = reduce_cameras(to_cameras(stacked, cam_index, total_cams))
    gradient = summed[:9]
    diagonal = summed[9:] + DAMPING
    residual = gradient
    precond = residual / diagonal
    direction = precond
    rz_now = inner_product(residual, precond)
    solution = jnp.zeros_like(gradient)
    for iteration in range(ITERS):
        whole = gather_cameras(direction)
        cam_values = jnp.take(whole, cam_index, axis=1)
        terms = to_cameras(schur_obs(cam_jac, lm_jac, inverse, cam_values), cam_index, total_cams)
        image = reduce_cameras(terms) + DAMPING * direction
        alpha = rz_now / inner_product(direction, image)
        solution = solution + alpha * direction
        residual = residual - alpha * image
        if iteration + 1 < ITERS:
            precond = residual / diagonal
            rz_next = inner_product(residual, precond)
            direction = precond + rz_next / rz_now * direction
            rz_now = rz_next
    whole_step = gather_cameras(solution)
    cam_obs = camera_apply(cam_jac, jnp.take(whole_step, cam_index, axis=1))
    landmark_step = land_rhs - apply_inverse(inverse, landmark_side(lm_jac, cam_obs))
    return (solution, residual, landmark_step)


def solution(mesh):
    in_specs = (
        P(None, None, None, ("group", "dev")),
        P(None, None, None, ("group", "dev")),
        P(None, None, ("group", "dev")),
        P(None, ("group", "dev")),
    )
    out_specs = (P(None, "dev"), P(None, "dev"), P(None, ("group", "dev")))
    return jax.shard_map(body, mesh=mesh, in_specs=in_specs, out_specs=out_specs, check_vma=False)
```

profile of v0, /device:TPU:8, one launch (start us, length us, event | category | flops | bytes accessed | tf_op | source)
XLA Modules:
  0.0 2390.0 jit_solution(14837299796872105308)
XLA Ops:
  7.2 0.8 multiply_reduce_fusion.22
  8.0 0.9 multiply_reduce_fusion.13
  9.0 0.7 copy.31
  9.8 0.9 multiply_reduce_fusion.12
  10.7 0.8 sub.128
  11.5 1.0 multiply_reduce_fusion.6
  13.2 24.5 %scatter_custom_fusion = f32[18,8192]{0,1:T(8,128)} fusion(s32[4096]{0:T(1024)S(1)} %bitcast.43, f32[4096,18]{1,0:T(8,128)S(1)} %bitcast.38, f32[]{:T(128)} %constant.14.clone.1), kind=kCustom, calls=%fused_computation.13 | custom fusion | flops 73728 | bytes 589828 | tf_op jit(solution)/shard_map/vmap()/scatter-add | solution.py:62
  37.9 494.2 %all-reduce.5.cloned.1.call-done = f32[18,8192]{0,1:T(8,128)} async-done(((f32[18,8192]{0,1:T(8,128)}), f32[18,8192]{0,1:T(8,128)}) %all-reduce.5.cloned.1.call-update) | async-done | bytes 589840 | tf_op jit(solution)/shard_map/psum | solution.py:78
  532.1 1.0 fusion.7
  533.1 111.9 %all_gather.9 = f32[9,8192]{0,1:T(8,128)} all-gather(f32[9,128]{0,1:T(8,128)S(1)} %fusion.7), channel_id=1, replica_groups=mesh['group'=8,'dev'=64] {'dev'}, dimensions={1}, use_global_device_ids=true | all-gather | bytes 299520 | tf_op jit(solution)/shard_map/all_gather | solution.py:74
  645.0 16.3 gather_fusion
  661.3 1.9 select_bitcast_fusion.2
  664.8 24.5 %scatter_custom_fusion.1 = f32[9,8192]{0,1:T(8,128)} fusion(s32[4096]{0:T(1024)S(1)} %bitcast.44, f32[4096,9]{1,0:T(8,128)S(1)} %bitcast.40, f32[]{:T(128)} %constant.14.clone.1), kind=kCustom, calls=%fused_computation.11 | custom fusion | flops 36864 | bytes 294916 | tf_op jit(solution)/shard_map/vmap()/scatter-add | solution.py:62
  689.4 488.0 %all-reduce.7.cloned.1.call-done = f32[9,8192]{0,1:T(8,128)} async-done(((f32[9,8192]{0,1:T(8,128)}), f32[9,8192]{0,1:T(8,128)}) %all-reduce.7.cloned.1.call-update) | async-done | bytes 294928 | tf_op jit(solution)/shard_map/psum | solution.py:78
  1177.4 1.6 multiply_reduce_fusion.16
  1179.0 139.5 %all-reduce = (f32[]{:T(128)}, f32[]{:T(128)}) all-reduce(f32[]{:T(128)} %get-tuple-element.22, f32[]{:T(128)} %get-tuple-element.21), channel_id=1, replica_groups=mesh['group'=8,'dev'=64] {'dev'}, use_global_device_ids=true, to_apply=%region_14.0 | all-reduce | flops 2 | bytes 16 | tf_op jit(solution)/shard_map/psum | solution.py:84
  1319.8 1.6 multiply_reduce_fusion.15
  1321.4 140.7 %psum.53 = f32[]{:T(128)} all-reduce(f32[]{:T(128)} %get-tuple-element.25), channel_id=1, replica_groups=mesh['group'=8,'dev'=64] {'dev'}, use_global_device_ids=true, to_apply=%region_25.27 | all-reduce | flops 1 | bytes 8 | tf_op jit(solution)/shard_map/psum | solution.py:84
  1463.5 1.0 multiply_add_fusion.1
  1464.5 110.5 %all_gather.10 = f32[9,8192]{0,1:T(8,128)} all-gather(f32[9,128]{0,1:T(8,128)S(1)} %multiply_add_fusion.1), channel_id=1, replica_groups=mesh['group'=8,'dev'=64] {'dev'}, dimensions={1}, use_global_device_ids=true | all-gather | bytes 299520 | tf_op jit(solution)/shard_map/all_gather | solution.py:74
  1575.0 16.3 gather_fusion.1
  1591.2 1.9 select_bitcast_fusion.1
  1594.6 24.5 %scatter_custom_fusion.2 = f32[9,8192]{0,1:T(8,128)} fusion(s32[4096]{0:T(1024)S(1)} %bitcast.45, f32[4096,9]{1,0:T(8,128)S(1)} %bitcast.39, f32[]{:T(128)} %constant.14.clone.1), kind=kCustom, calls=%fused_computation.9 | custom fusion | flops 36864 | bytes 294916 | tf_op jit(solution)/shard_map/vmap()/scatter-add | solution.py:62
  1619.2 488.2 %all-reduce.9.cloned.1.call-done = f32[9,8192]{0,1:T(8,128)} async-done(((f32[9,8192]{0,1:T(8,128)}), f32[9,8192]{0,1:T(8,128)}) %all-reduce.9.cloned.1.call-update) | async-done | bytes 294928 | tf_op jit(solution)/shard_map/psum | solution.py:78
  2107.4 1.5 multiply_reduce_fusion.14
  2108.9 139.4 %psum.55 = f32[]{:T(128)} all-reduce(f32[]{:T(128)} %multiply_reduce_fusion.14), channel_id=1, replica_groups=mesh['group'=8,'dev'=64] {'dev'}, use_global_device_ids=true, to_apply=%region_34.36 | all-reduce | flops 1 | bytes 8 | tf_op jit(solution)/shard_map/psum | solution.py:84
  2249.7 1.0 multiply_subtract_fusion
  2250.7 0.7 copy.26
  2251.4 111.8 %all_gather.11 = f32[9,8192]{0,1:T(8,128)} all-gather(f32[9,128]{0,1:T(8,128)S(1)} %get-tuple-element.34), channel_id=1, replica_groups=mesh['group'=8,'dev'=64] {'dev'}, dimensions={1}, use_global_device_ids=true | all-gather | bytes 299520 | tf_op jit(solution)/shard_map/all_gather | solution.py:74
  2363.2 0.7 copy.27
  2363.9 16.3 gather_fusion.2
  2380.2 1.9 select_bitcast_fusion
  (42 shorter events, 5.1 us)
Async XLA Ops:
  7.2 524.9 %all-reduce.5.cloned.1.call-start = ((), (), s32[]{:S(2)}) async-start(), calls=%async_computation | async-start | bytes 8388608 | tf_op jit(solution)/shard_map/psum | solution.py:78
  13.2 24.6 %copy-start.2 = (s32[8,512]{1,0:T(8,128)S(1)}, s32[8,512]{1,0:T(8,128)}, u32[]{:S(2)}) copy-start(s32[8,512]{1,0:T(8,128)} %param.9) | copy-start | bytes 49156
  37.8 1139.6 %all-reduce.7.cloned.1.call-start = ((), (), s32[]{:S(2)}) async-start(), calls=%async_computation.1 | async-start | bytes 8388608 | tf_op jit(solution)/shard_map/psum | solution.py:78
  645.0 18.9 copy-start
  645.0 19.0 copy-start.1
  689.3 1418.1 %all-reduce.9.cloned.1.call-start = ((), (), s32[]{:S(2)}) async-start(), calls=%async_computation.2 | async-start | bytes 8388608 | tf_op jit(solution)/shard_map/psum | solution.py:78
Sparse Core Ops, SparseCore 0:
  37.9 494.1 all-reduce.4
  689.4 487.8 all-reduce.6
  1619.3 488.0 all-reduce.8
where the time goes:
time: 2390 us
  waiting for transfers between devices  1470 us (62%)
  blocking collectives  754 us (32%)
  other arithmetic  92.8 us (4%)
  local copies, waits for them, and re-layouts  54.8 us (2%)
    psum x3, waiting for transfers between devices, reduce_cameras(): totals = lax.psum(terms, ('group', 'dev'))  1470 us
    psum x3, blocking collectives, inner_product(): return lax.psum(jnp.sum(left * right), 'dev')  420 us
    all_gather x3, blocking collectives, gather_cameras(): return lax.all_gather(tile, 'dev', axis=1, tiled=True)  334 us
    scatter-add x3, other arithmetic, one_row(): return jax.ops.segment_sum(column, flat_index, num_segments=total_cams)  73.6 us
  transfers between devices with their start and end apart: 3, of which 3 were waited for; matrix products, arithmetic and copies ran while one was open for 0% of the time, Pallas kernels for 0%

commit v1 on v0

--- a/solution.py
+++ b/solution.py
@@ -75,7 +75,8 @@
 
 
 def reduce_cameras(terms):
-    totals = lax.psum(terms, ("group", "dev"))
+    half = lax.psum(terms, "dev")
+    totals = lax.psum(half, "group")
     width = terms.shape[1] // lax.axis_size("dev")
     return lax.dynamic_slice_in_dim(totals, lax.axis_index("dev") * width, width, 1)
 

time: 2390 us -> 2050 us (0.86)
  waiting for transfers between devices: 1470 us -> 1120 us
    psum x3 -> x6, waiting for transfers between devices: 1470 us -> 1120 us  [the longest x3 861 us: reduce_cameras(): half = lax.psum(terms, 'dev')]
  transfers between devices with their start and end apart: 3 -> 6, of which waited for: 3 -> 6; matrix products, arithmetic and copies ran while one was open for 0% -> 0% of each run, Pallas kernels for 0% -> 0%
where the time goes in v1:
time: 2050 us
  waiting for transfers between devices  1120 us (55%)
  blocking collectives  765 us (37%)
  other arithmetic  92.7 us (5%)
  local copies, waits for them, and re-layouts  54.8 us (3%)
    psum x3, waiting for transfers between devices, reduce_cameras(): half = lax.psum(terms, 'dev')  861 us
    psum x3, blocking collectives, inner_product(): return lax.psum(jnp.sum(left * right), 'dev')  425 us
    all_gather x3, blocking collectives, gather_cameras(): return lax.all_gather(tile, 'dev', axis=1, tiled=True)  340 us
    psum x3, waiting for transfers between devices, reduce_cameras(): totals = lax.psum(half, 'group')  259 us
    scatter-add x3, other arithmetic, one_row(): return jax.ops.segment_sum(column, flat_index, num_segments=total_cams)  73.6 us
  transfers between devices with their start and end apart: 6, of which 6 were waited for; matrix products, arithmetic and copies ran while one was open for 0% of the time, Pallas kernels for 0%

profile of v1, /device:TPU:8, one launch (start us, length us, event | category | flops | bytes accessed | tf_op | source)
XLA Modules:
  0.0 2051.0 jit_solution(17932854570305599346)
XLA Ops:
  7.2 0.8 multiply_reduce_fusion.22
  8.0 0.9 multiply_reduce_fusion.13
  9.8 0.9 multiply_reduce_fusion.12
  10.7 0.8 sub.128
  11.5 1.0 multiply_reduce_fusion.6
  13.2 24.5 %scatter_custom_fusion = f32[18,8192]{0,1:T(8,128)} fusion(s32[4096]{0:T(1024)S(1)} %bitcast.43, f32[4096,18]{1,0:T(8,128)S(1)} %bitcast.38, f32[]{:T(128)} %constant.14.clone.1), kind=kCustom, calls=%fused_computation.13 | custom fusion | flops 73728 | bytes 589828 | tf_op jit(solution)/shard_map/vmap()/scatter-add | solution.py:62
  37.8 292.9 %all-reduce.8.cloned.1.call-done = f32[18,8192]{0,1:T(8,128)} async-done(((f32[18,8192]{0,1:T(8,128)}), f32[18,8192]{0,1:T(8,128)}) %all-reduce.8.cloned.1.call-update) | async-done | bytes 589840 | tf_op jit(solution)/shard_map/psum | solution.py:78
  330.8 86.4 %all-reduce.10.cloned.1.call-done = f32[18,8192]{0,1:T(8,128)} async-done(((f32[18,8192]{0,1:T(8,128)}), f32[18,8192]{0,1:T(8,128)}) %all-reduce.10.cloned.1.call-update) | async-done | bytes 589840 | tf_op jit(solution)/shard_map/psum | solution.py:79
  417.2 1.0 fusion.7
  418.2 115.0 %all_gather.9 = f32[9,8192]{0,1:T(8,128)} all-gather(f32[9,128]{0,1:T(8,128)S(1)} %fusion.7), channel_id=1, replica_groups=mesh['group'=8,'dev'=64] {'dev'}, dimensions={1}, use_global_device_ids=true | all-gather | bytes 299520 | tf_op jit(solution)/shard_map/all_gather | solution.py:74
  533.2 16.3 gather_fusion
  549.5 1.9 select_bitcast_fusion.2
  553.0 24.5 %scatter_custom_fusion.1 = f32[9,8192]{0,1:T(8,128)} fusion(s32[4096]{0:T(1024)S(1)} %bitcast.44, f32[4096,9]{1,0:T(8,128)S(1)} %bitcast.40, f32[]{:T(128)} %constant.14.clone.1), kind=kCustom, calls=%fused_computation.11 | custom fusion | flops 36864 | bytes 294916 | tf_op jit(solution)/shard_map/vmap()/scatter-add | solution.py:62
  577.6 284.1 %all-reduce.12.cloned.1.call-done = f32[9,8192]{0,1:T(8,128)} async-done(((f32[9,8192]{0,1:T(8,128)}), f32[9,8192]{0,1:T(8,128)}) %all-reduce.12.cloned.1.call-update) | async-done | bytes 294928 | tf_op jit(solution)/shard_map/psum | solution.py:78
  861.8 86.3 %all-reduce.14.cloned.1.call-done = f32[9,8192]{0,1:T(8,128)} async-done(((f32[9,8192]{0,1:T(8,128)}), f32[9,8192]{0,1:T(8,128)}) %all-reduce.14.cloned.1.call-update) | async-done | bytes 294928 | tf_op jit(solution)/shard_map/psum | solution.py:79
  948.1 1.6 multiply_reduce_fusion.16
  949.7 140.8 %all-reduce = (f32[]{:T(128)}, f32[]{:T(128)}) all-reduce(f32[]{:T(128)} %get-tuple-element.22, f32[]{:T(128)} %get-tuple-element.21), channel_id=1, replica_groups=mesh['group'=8,'dev'=64] {'dev'}, use_global_device_ids=true, to_apply=%region_15.0 | all-reduce | flops 2 | bytes 16 | tf_op jit(solution)/shard_map/psum | solution.py:85
  1091.8 1.6 multiply_reduce_fusion.15
  1093.5 143.2 %psum.76 = f32[]{:T(128)} all-reduce(f32[]{:T(128)} %get-tuple-element.25), channel_id=1, replica_groups=mesh['group'=8,'dev'=64] {'dev'}, use_global_device_ids=true, to_apply=%region_27.29 | all-reduce | flops 1 | bytes 8 | tf_op jit(solution)/shard_map/psum | solution.py:85
  1238.0 1.0 multiply_add_fusion.1
  1239.1 110.6 %all_gather.10 = f32[9,8192]{0,1:T(8,128)} all-gather(f32[9,128]{0,1:T(8,128)S(1)} %multiply_add_fusion.1), channel_id=1, replica_groups=mesh['group'=8,'dev'=64] {'dev'}, dimensions={1}, use_global_device_ids=true | all-gather | bytes 299520 | tf_op jit(solution)/shard_map/all_gather | solution.py:74
  1349.7 16.3 gather_fusion.1
  1365.9 1.9 select_bitcast_fusion.1
  1369.3 24.5 %scatter_custom_fusion.2 = f32[9,8192]{0,1:T(8,128)} fusion(s32[4096]{0:T(1024)S(1)} %bitcast.45, f32[4096,9]{1,0:T(8,128)S(1)} %bitcast.39, f32[]{:T(128)} %constant.14.clone.1), kind=kCustom, calls=%fused_computation.9 | custom fusion | flops 36864 | bytes 294916 | tf_op jit(solution)/shard_map/vmap()/scatter-add | solution.py:62
  1394.0 283.7 %all-reduce.16.cloned.1.call-done = f32[9,8192]{0,1:T(8,128)} async-done(((f32[9,8192]{0,1:T(8,128)}), f32[9,8192]{0,1:T(8,128)}) %all-reduce.16.cloned.1.call-update) | async-done | bytes 294928 | tf_op jit(solution)/shard_map/psum | solution.py:78
  1677.7 86.3 %all-reduce.18.cloned.1.call-done = f32[9,8192]{0,1:T(8,128)} async-done(((f32[9,8192]{0,1:T(8,128)}), f32[9,8192]{0,1:T(8,128)}) %all-reduce.18.cloned.1.call-update) | async-done | bytes 294928 | tf_op jit(solution)/shard_map/psum | solution.py:79
  1764.0 1.5 multiply_reduce_fusion.14
  1765.5 140.8 %psum.79 = f32[]{:T(128)} all-reduce(f32[]{:T(128)} %multiply_reduce_fusion.14), channel_id=1, replica_groups=mesh['group'=8,'dev'=64] {'dev'}, use_global_device_ids=true, to_apply=%region_37.39 | all-reduce | flops 1 | bytes 8 | tf_op jit(solution)/shard_map/psum | solution.py:85
  1907.7 1.0 multiply_subtract_fusion
  1909.4 114.5 %all_gather.11 = f32[9,8192]{0,1:T(8,128)} all-gather(f32[9,128]{0,1:T(8,128)S(1)} %get-tuple-element.34), channel_id=1, replica_groups=mesh['group'=8,'dev'=64] {'dev'}, dimensions={1}, use_global_device_ids=true | all-gather | bytes 299520 | tf_op jit(solution)/shard_map/all_gather | solution.py:74
  2024.6 16.3 gather_fusion.2
  2040.8 1.9 select_bitcast_fusion
  (51 shorter events, 7.3 us)
Async XLA Ops:
  7.2 323.5 %all-reduce.8.cloned.1.call-start = ((), (), s32[]{:S(2)}) async-start(), calls=%async_computation | async-start | bytes 8388608 | tf_op jit(solution)/shard_map/psum | solution.py:78
  13.2 24.6 %copy-start.2 = (s32[8,512]{1,0:T(8,128)S(1)}, s32[8,512]{1,0:T(8,128)}, u32[]{:S(2)}) copy-start(s32[8,512]{1,0:T(8,128)} %param.9) | copy-start | bytes 49156
  37.7 379.5 %all-reduce.10.cloned.1.call-start = ((), (), s32[]{:S(2)}) async-start(), calls=%async_computation.1 | async-start | bytes 8388608 | tf_op jit(solution)/shard_map/psum | solution.py:79
  330.7 531.0 %all-reduce.12.cloned.1.call-start = ((), (), s32[]{:S(2)}) async-start(), calls=%async_computation.2 | async-start | bytes 8388608 | tf_op jit(solution)/shard_map/psum | solution.py:78
  533.2 18.9 copy-start
  533.2 19.0 copy-start.1
  577.5 370.5 %all-reduce.14.cloned.1.call-start = ((), (), s32[]{:S(2)}) async-start(), calls=%async_computation.3 | async-start | bytes 8388608 | tf_op jit(solution)/shard_map/psum | solution.py:79
  861.7 815.9 %all-reduce.16.cloned.1.call-start = ((), (), s32[]{:S(2)}) async-start(), calls=%async_computation.4 | async-start | bytes 8388608 | tf_op jit(solution)/shard_map/psum | solution.py:78
  1393.9 370.1 %all-reduce.18.cloned.1.call-start = ((), (), s32[]{:S(2)}) async-start(), calls=%async_computation.5 | async-start | bytes 8388608 | tf_op jit(solution)/shard_map/psum | solution.py:79
Sparse Core Ops, SparseCore 0:
  37.8 292.8 all-reduce.7
  333.0 84.0 all-reduce.9
  577.7 284.0 all-reduce.11
  863.9 84.0 all-reduce.13
  1394.0 283.6 all-reduce.15
  1679.9 84.0 all-reduce.17
